TPU v7x, 128 devices: a whole 4x4x4 slice. The times are simulated.
128 devices in a mesh: pix: 16 (over x, y_hi, core), tm: 8 (over y_lo, z).
Axes of the slice: x: 4, y: 4 (y_hi: 2, y_lo: 2; y = y_hi * 2 + y_lo), z: 4, core: 2. Of those that a mesh axis runs over, the one named last changes fastest.
Arguments:
- movie: bfloat16 [32768, 8192], P('pix', 'tm'), may hold values from -6 to 6
- offsets: int32 [8], replicated, may hold values from -129 to 129, as said below
- spatial: bfloat16 [512, 32768], P('tm', 'pix'), may hold values from -6 to 6
- temporal: bfloat16 [512, 8192], P('pix', 'tm'), may hold values from -6 to 6
- step_spatial: float32 [512], replicated, may hold values from 0.3 to 1
- step_temporal: float32 [512], replicated, may hold values from 0.3 to 1
- thresh_spatial: float32 [512], replicated, may hold values from 0.01 to 0.2
- thresh_temporal: float32 [512], replicated, may hold values from 0.01 to 0.2
Outputs:
- spatial_out: bfloat16 [512, 32768], P('tm', 'pix')
- temporal_out: bfloat16 [512, 8192], P('pix', 'tm')
Inputs may be any that keep to these rules, and one draw needn't show every extreme that they name: `offsets`: every offset is a nonzero pixel step of magnitude at most 129; both 129 and -129 occur among them.
All inputs are finite; a program needn't handle non-finite values.
Results may differ from a plain program's by a relative error of at most 0.0052.
Values may be sent and summed in bfloat16 or wider, within the bound.
No kernel may reach another device: no remote copies, remote signals or barrier semaphores. Data moves between devices by JAX's collectives and lax.ppermute only.
A program may use at most 64 MiB of HBM per device.

v0:
```python
import math
import jax
import jax.numpy as jnp
from jax import lax
from jax.sharding import PartitionSpec as P

HALO = 129
NBR = 8
ROUNDS = 2


def padded_2(array, sides, width):
    for axis, dim in sides:
        size, length = (lax.axis_size(axis), array.shape[dim])
        up = [(i, (i + 1) % size) for i in range(size - 1)]
        down = [(j, i) for i, j in up]
        last = lax.slice_in_dim(array, length - width, length, axis=dim)
        initial = lax.slice_in_dim(array, 0, width, axis=dim)
        before = lax.ppermute(last, axis, up)
        after = lax.ppermute(initial, axis, down)
        array = jnp.concatenate([before, array, after], axis=dim)
    return array


def soften(values, limit):
    return values - jnp.clip(values, -limit, limit)


def contrast(movie, offsets):
    count = movie.shape[0]
    padded = padded_2(movie, (("pix", 0),), HALO)
    total = jnp.zeros(movie.shape, jnp.float32)
    for neighbour in range(NBR):
        begin = HALO + offsets[neighbour]
        shifted = lax.dynamic_slice_in_dim(padded, begin, count, 0)
        total = total + shifted.astype(jnp.float32)
    return (movie.astype(jnp.float32) - total / NBR).astype(jnp.bfloat16)


def residual(contrasted, spatial_full, temporal_full, rank):
    model = lax.dot_general(
        spatial_full, temporal_full, (((0,), (0,)), ((), ())), preferred_element_type=jnp.float32
    )
    return (contrasted.astype(jnp.float32) - model * (1.0 / math.sqrt(rank))).astype(jnp.bfloat16)


def per_device(
    movie, offsets, spatial, temporal, step_spatial, step_temporal, thresh_spatial, thresh_temporal
):
    spatial_rows = spatial.shape[0]
    temporal_rows = temporal.shape[0]
    rank = spatial_rows * lax.axis_size("tm")
    pixels = movie.shape[0] * lax.axis_size("pix")
    frames = movie.shape[1] * lax.axis_size("tm")
    contrasted = contrast(movie, offsets)
    spatial_full = lax.all_gather(spatial, "tm", axis=0, tiled=True)
    temporal_full = lax.all_gather(temporal, "pix", axis=0, tiled=True)
    coef_temporal = step_temporal * (math.sqrt(rank) / pixels)
    coef_spatial = step_spatial * (math.sqrt(rank) / frames)
    temporal_first = lax.axis_index("pix") * temporal_rows
    spatial_first = lax.axis_index("tm") * spatial_rows
    for turn in range(ROUNDS):
        errors = residual(contrasted, spatial_full, temporal_full, rank)
        grad_temporal = lax.psum(
            jnp.dot(spatial_full, errors, preferred_element_type=jnp.float32), "pix"
        )
        temporal_full = soften(
            temporal_full.astype(jnp.float32) + coef_temporal[:, None] * grad_temporal,
            thresh_temporal[:, None],
        ).astype(jnp.bfloat16)
        errors = residual(contrasted, spatial_full, temporal_full, rank)
        partial_spatial = lax.dot_general(
            temporal_full, errors, (((1,), (1,)), ((), ())), preferred_element_type=jnp.float32
        )
        grad_spatial = lax.psum(partial_spatial, "tm")
        spatial_full = soften(
            spatial_full.astype(jnp.float32) + coef_spatial[:, None] * grad_spatial,
            thresh_spatial[:, None],
        ).astype(jnp.bfloat16)
    spatial_out = lax.dynamic_slice_in_dim(spatial_full, spatial_first, spatial_rows, 0)
    temporal_out = lax.dynamic_slice_in_dim(temporal_full, temporal_first, temporal_rows, 0)
    return (spatial_out, temporal_out)


def solution(mesh):
    placed = (P("pix", "tm"), P(), P("tm", "pix"), P("pix", "tm"), P(), P(), P(), P())
    return jax.shard_map(
        per_device,
        mesh=mesh,
        in_specs=placed,
        out_specs=(P("tm", "pix"), P("pix", "tm")),
        check_vma=False,
    )
```

profile of v0, /device:TPU:1, one launch (start us, length us, event | category | flops | bytes accessed | tf_op | source)
XLA Modules:
  0.0 656.8 jit_solution(3651057395726386924)
XLA Ops:
  7.2 0.0 all-gather.5.cloned.1.call-start
  7.2 0.7 all-gather.5.cloned.1.call-update
  7.9 0.0 all-gather.3.cloned.1.call-start
  7.9 0.7 all-gather.3.cloned.1.call-update
  8.6 0.0 all-reduce.5.cloned.1.call-start
  8.7 1.1 fusion.12
  9.8 6.2 collective-permute-start
  16.0 1.9 collective-permute-start.1
  18.0 1.6 fusion.13
  29.6 0.0 collective-permute-done
  29.6 0.0 collective-permute-done.1
  29.6 24.4 %concatenate.3 = bf16[2306,1024]{1,0:T(8,128)(2,1)} concatenate(bf16[129,1024]{1,0:T(8,128)(2,1)S(1)} %collective-permute-done, bf16[2048,1024]{1,0:T(8,128)(2,1)} %param.8, bf16[129,1024]{1,0:T(8,128)(2,1)S(1)} %collective-permute-done.1), dimensions={0} | concatenate | bytes 9445376 | tf_op jit(solution)/shard_map/concatenate | solution.py:21
  54.0 19.6 %subtract_convert_fusion = bf16[2048,1024]{1,0:T(8,128)(2,1)} fusion(bf16[2048,1024]{1,0:T(8,128)(2,1)} %param.8, bf16[2306,1024]{1,0:T(8,128)(2,1)} %concatenate.3, s32[]{:T(128)S(6)} %select_n.37, s32[]{:T(128)S(6)} %select_n.36, s32[]{:T(128)S(6)} %select_n.35, s32[]{:T(128)S(6)} %select_n.34, s32[]{:T(128)S(6)} %select_n.33, s32[]{:T(128)S(6)} %select_n.32, ...), kind=kLoop, calls=%fused_computation.8 | loop fusion | flops 39845888 | bytes 41943072 | tf_op jit(solution)/shard_map/convert_element_type | solution.py:37
  73.6 0.0 copy-start.1
  73.6 0.0 copy-start.3
  73.6 0.0 all-gather.5.cloned.1.call-done
  73.6 0.0 copy-start
  73.6 21.8 %all-gather.3.cloned.1.call-done = bf16[512,2048]{1,0:T(8,128)(2,1)} async-done(((bf16[64,2048]{1,0:T(8,128)(2,1)}), bf16[512,2048]{1,0:T(8,128)(2,1)}) %all-gather.3.cloned.1.call-update) | async-done | bytes 2097168 | tf_op jit(solution)/shard_map/all_gather | solution.py:56
  95.5 9.9 %convolution_bitcast_fusion = f32[512,1024]{0,1:T(8,128)} fusion(bf16[512,2048]{1,0:T(8,128)(2,1)} %all-gather.3.cloned.1.call-done, bf16[2048,1024]{1,0:T(8,128)(2,1)} %subtract_convert_fusion, bf16[512,1024]{1,0:T(8,128)(2,1)} %all-gather.5.cloned.1.call-done), kind=kOutput, calls=%fused_computation.12 | convolution fusion | flops 4303355904 | bytes 9437184 | tf_op jit(solution)/shard_map/dot_general | solution.py:65
  105.4 0.0 all-reduce.5.cloned.1.call-update
  105.4 0.2 all-reduce.7.cloned.1.call-start
  105.6 0.0 copy-done.1
  105.6 0.0 copy-done.3
  105.7 0.0 copy-done
  105.7 0.5 copy.13
  106.2 147.7 %all-reduce.5.cloned.1.call-done = f32[512,1024]{0,1:T(8,128)} async-done(((f32[512,1024]{0,1:T(8,128)}), f32[512,1024]{0,1:T(8,128)}) %all-reduce.5.cloned.1.call-update) | async-done | bytes 2097168 | tf_op jit(solution)/shard_map/psum | solution.py:64
  254.0 2.1 subtract_convert_fusion.3
  256.0 9.8 %fusion.6 = f32[512,2048]{1,0:T(8,128)} fusion(bf16[512,1024]{0,1:T(8,128)(2,1)S(1)} %subtract_convert_fusion.3, bf16[2048,1024]{1,0:T(8,128)(2,1)} %subtract_convert_fusion, bf16[512,2048]{1,0:T(8,128)(2,1)} %all-gather.3.cloned.1.call-done), kind=kOutput, calls=%fused_computation.15 | convolution fusion | flops 4303355904 | bytes 11534336 | tf_op jit(solution)/shard_map/dot_general | solution.py:72
  265.8 0.0 copy-start.2
  265.8 0.0 copy-start.4
  265.8 0.0 all-reduce.7.cloned.1.call-update
  265.9 0.0 all-reduce.9.cloned.1.call-start
  265.9 0.6 copy-done.2
  266.5 0.0 copy-done.4
  266.5 106.3 %all-reduce.7.cloned.1.call-done = f32[512,2048]{1,0:T(8,128)} async-done(((f32[512,2048]{1,0:T(8,128)}), f32[512,2048]{1,0:T(8,128)}) %all-reduce.7.cloned.1.call-update) | async-done | bytes 4194320 | tf_op jit(solution)/shard_map/psum | solution.py:75
  372.9 3.9 subtract_convert_fusion.1
  376.7 8.5 %fusion.5 = f32[512,1024]{0,1:T(8,128)} fusion(bf16[512,2048]{1,0:T(8,128)(2,1)S(1)} %subtract_convert_fusion.1, bf16[2048,1024]{1,0:T(8,128)(2,1)} %subtract_convert_fusion, bf16[512,1024]{0,1:T(8,128)(2,1)S(1)} %subtract_convert_fusion.3), kind=kOutput, calls=%fused_computation.14 | convolution fusion | flops 4303355904 | bytes 9437184 | tf_op jit(solution)/shard_map/dot_general | solution.py:65
  385.2 0.0 all-reduce.9.cloned.1.call-update
  385.3 0.3 all-reduce.11.cloned.1.call-start
  385.5 142.7 %all-reduce.9.cloned.1.call-done = f32[512,1024]{0,1:T(8,128)} async-done(((f32[512,1024]{0,1:T(8,128)}), f32[512,1024]{0,1:T(8,128)}) %all-reduce.9.cloned.1.call-update) | async-done | bytes 2097168 | tf_op jit(solution)/shard_map/psum | solution.py:64
  528.2 3.0 subtract_convert_fusion.2
  531.3 9.7 %fusion.4 = f32[512,2048]{1,0:T(8,128)} fusion(bf16[512,1024]{0,1:T(8,128)(2,1)} %subtract_convert_fusion.2, bf16[2048,1024]{1,0:T(8,128)(2,1)} %subtract_convert_fusion, bf16[512,2048]{1,0:T(8,128)(2,1)S(1)} %subtract_convert_fusion.1), kind=kOutput, calls=%fused_computation.13 | convolution fusion | flops 4303355904 | bytes 11534336 | tf_op jit(solution)/shard_map/dot_general | solution.py:72
  541.0 0.0 all-reduce.11.cloned.1.call-update
  541.0 0.1 dynamic-slice
  541.1 0.1 dynamic-slice.1
  541.2 0.1 dynamic-slice.2
  541.3 1.1 constant_dynamic-slice_fusion
  542.3 0.8 copy.15
  543.1 105.0 %all-reduce.11.cloned.1.call-done = f32[512,2048]{1,0:T(8,128)} async-done(((f32[512,2048]{1,0:T(8,128)}), f32[512,2048]{1,0:T(8,128)}) %all-reduce.11.cloned.1.call-update) | async-done | bytes 4194320 | tf_op jit(solution)/shard_map/psum | solution.py:75
  648.1 1.9 subtract_convert_fusion.4
  (4 shorter events, 0.0 us)
Async XLA Ops:
  7.2 66.4 %all-gather.5.cloned.1.call-start = ((), (), s32[]{:S(2)}) async-start(), calls=%async_computation.1 | async-start | bytes 1114112 | tf_op jit(solution)/shard_map/all_gather | solution.py:57
  7.9 87.6 %all-gather.3.cloned.1.call-start = ((), (), s32[]{:S(2)}) async-start(), calls=%async_computation | async-start | bytes 2359296 | tf_op jit(solution)/shard_map/all_gather | solution.py:56
  8.6 245.3 %all-reduce.5.cloned.1.call-start = ((), (), s32[]{:S(2)}) async-start(), calls=%async_computation.2 | async-start | bytes 4194304 | tf_op jit(solution)/shard_map/psum | solution.py:64
  9.8 19.8 %collective-permute-start = (bf16[129,1024]{1,0:T(8,128)(2,1)S(1)}, bf16[129,1024]{1,0:T(8,128)(2,1)S(1)}, u32[]{:S(2)}, u32[]{:S(2)}) collective-permute-start(bf16[129,1024]{1,0:T(8,128)(2,1)S(1)} %get-tuple-element.7), channel_id=1, source_target_pairs={{0,8},{8,16},{16,24},{24,32},{32,40},{40,48},{48,56},{56,64},{64,7... | collective-permute-start | bytes 792584 | tf_op jit(solution)/shard_map/ppermute | solution.py:19
  16.0 13.5 %collective-permute-start.1 = (bf16[129,1024]{1,0:T(8,128)(2,1)S(1)}, bf16[129,1024]{1,0:T(8,128)(2,1)S(1)}, u32[]{:S(2)}, u32[]{:S(2)}) collective-permute-start(bf16[129,1024]{1,0:T(8,128)(2,1)S(1)} %get-tuple-element.6), channel_id=1, source_target_pairs={{8,0},{16,8},{24,16},{32,24},{40,32},{48,40},{56,48},{64,56},{72,6... | collective-permute-start | bytes 792584 | tf_op jit(solution)/shard_map/ppermute | solution.py:20
  73.6 32.1 %copy-start.1 = (f32[512]{0:T(512)S(1)}, f32[512]{0:T(512)}, u32[]{:S(2)}) copy-start(f32[512]{0:T(512)} %param.15) | copy-start | bytes 6148
  73.6 32.1 %copy-start.3 = (f32[512]{0:T(512)S(1)}, f32[512]{0:T(512)}, u32[]{:S(2)}) copy-start(f32[512]{0:T(512)} %param.13) | copy-start | bytes 6148
  73.6 32.1 %copy-start = (bf16[512,1024]{1,0:T(8,128)(2,1)S(1)}, bf16[512,1024]{1,0:T(8,128)(2,1)}, u32[]{:S(2)}) copy-start(bf16[512,1024]{1,0:T(8,128)(2,1)} %all-gather.5.cloned.1.call-done) | copy-start | bytes 3145732
  105.4 267.5 %all-reduce.7.cloned.1.call-start = ((), (), s32[]{:S(2)}) async-start(), calls=%async_computation.3 | async-start | bytes 8388608 | tf_op jit(solution)/shard_map/psum | solution.py:75
  265.8 0.7 copy-start.2
  265.8 0.7 copy-start.4
  265.9 262.4 %all-reduce.9.cloned.1.call-start = ((), (), s32[]{:S(2)}) async-start(), calls=%async_computation.4 | async-start | bytes 4194304 | tf_op jit(solution)/shard_map/psum | solution.py:64
  385.3 262.8 %all-reduce.11.cloned.1.call-start = ((), (), s32[]{:S(2)}) async-start(), calls=%async_computation.5 | async-start | bytes 8388608 | tf_op jit(solution)/shard_map/psum | solution.py:75
Sparse Core Ops, SparseCore 0:
  10.4 48.5 all-gather.4
  60.6 34.7 all-gather.2
  105.5 148.3 all-reduce.4
  266.0 106.8 all-reduce.6
  385.4 142.8 all-reduce.8
  541.1 106.8 all-reduce.10
where the time goes:
time: 658 us; the launch traced here: 657 us
  waiting for transfers between devices  525 us (80%)
  matrix products  37.9 us (6%)
  local copies, waits for them, and re-layouts  30.4 us (5%)
  other arithmetic  30.4 us (5%)
  between operations  24.2 us (4%)
  starting transfers between devices  8.77 us (1%)
    psum x2, waiting for transfers between devices, per_device(): lax.psum(jnp.dot(spatial_full, errors, preferred_element_type=jnp.float32...  290 us
    psum x2, waiting for transfers between devices, per_device(): grad_spatial = lax.psum(partial_spatial, 'tm')  211 us
    concatenate x1, local copies, waits for them, and re-layouts, padded_2(): array = jnp.concatenate([before, array, after], axis=dim)  24.4 us
    all_gather x1, waiting for transfers between devices, per_device(): spatial_full = lax.all_gather(spatial, 'tm', axis=0, tiled=True)  21.8 us
    convert_element_type x1, other arithmetic, contrast(): return (movie.astype(jnp.float32) - total / NBR).astype(jnp.bfloat16)  19.6 us
    dot_general x2, matrix products, per_device(): lax.dot_general(temporal_full, errors, (((1,), (1,)), ((), ())), preferre...  19.5 us
    dot_general x2, matrix products, per_device(): jnp.dot(spatial_full, errors, preferred_element_type=jnp.float32)  18.4 us
  transfers between devices with their start and end apart: 8, of which 5 were waited for; matrix products, arithmetic and copies ran while one was open for 8% of the time, Pallas kernels for 0%

commit v1 on v0

--- a/solution.py
+++ b/solution.py
@@ -61,8 +61,11 @@
     spatial_first = lax.axis_index("tm") * spatial_rows
     for turn in range(ROUNDS):
         errors = residual(contrasted, spatial_full, temporal_full, rank)
-        grad_temporal = lax.psum(
-            jnp.dot(spatial_full, errors, preferred_element_type=jnp.float32), "pix"
+        grad_temporal = jnp.sum(
+            lax.all_gather(
+                jnp.dot(spatial_full, errors, preferred_element_type=jnp.float32), "pix"
+            ),
+            axis=0,
         )
         temporal_full = soften(
             temporal_full.astype(jnp.float32) + coef_temporal[:, None] * grad_temporal,

time: 658 us -> 795 us (1.21)
  waiting for transfers between devices: 525 us -> 605 us
  local copies, waits for them, and re-layouts: 30.4 us -> 67 us
  other arithmetic: 30.4 us -> 49.4 us
    all_gather x0 -> x2, waiting for transfers between devices: none -> 379 us  [per_device(): lax.all_gather(jnp.dot(spatial_full, errors, preferred_element_type=jnp.f...]
    psum x2 -> x0, waiting for transfers between devices: 290 us -> none  [per_device(): lax.psum(jnp.dot(spatial_full, errors, preferred_element_type=jnp.float32...]
    unnamed x11 -> x16, local copies, waits for them, and re-layouts: 1.38 us -> 36.1 us
    reduce_sum x0 -> x2, other arithmetic: none -> 20.4 us  [per_device(): jnp.sum(lax.all_gather(jnp.dot(spatial_full, errors, preferred_element_ty...]
    psum x2, waiting for transfers between devices: 211 us -> 203 us  [per_device(): grad_spatial = lax.psum(partial_spatial, 'tm')]
  transfers between devices with their start and end apart: 8 -> 8, of which waited for: 5 -> 5; matrix products, arithmetic and copies ran while one was open for 8% -> 6% of each run, Pallas kernels for 0% -> 0%
where the time goes in v1:
time: 795 us; the launch traced here: 793 us
  waiting for transfers between devices  605 us (76%)
  local copies, waits for them, and re-layouts  67 us (8%)
  other arithmetic  49.4 us (6%)
  matrix products  38.9 us (5%)
  between operations  24 us (3%)
  starting transfers between devices  8.77 us (1%)
    all_gather x2, waiting for transfers between devices, per_device(): lax.all_gather(jnp.dot(spatial_full, errors, preferred_element_type=jnp.f...  379 us
    psum x2, waiting for transfers between devices, per_device(): grad_spatial = lax.psum(partial_spatial, 'tm')  203 us
    unnamed x16, local copies, waits for them, and re-layouts  36.1 us
    concatenate x1, local copies, waits for them, and re-layouts, padded_2(): array = jnp.concatenate([before, array, after], axis=dim)  24.5 us
    all_gather x1, waiting for transfers between devices, per_device(): spatial_full = lax.all_gather(spatial, 'tm', axis=0, tiled=True)  22.1 us
    reduce_sum x2, other arithmetic, per_device(): jnp.sum(lax.all_gather(jnp.dot(spatial_full, errors, preferred_element_ty...  20.4 us
    dot_general x2, matrix products, per_device(): lax.dot_general(temporal_full, errors, (((1,), (1,)), ((), ())), preferre...  19.6 us
    convert_element_type x1, other arithmetic, contrast(): return (movie.astype(jnp.float32) - total / NBR).astype(jnp.bfloat16)  19.5 us
  transfers between devices with their start and end apart: 8, of which 5 were waited for; matrix products, arithmetic and copies ran while one was open for 6% of the time, Pallas kernels for 0%

profile of v1, /device:TPU:1, one launch (start us, length us, event | category | flops | bytes accessed | tf_op | source)
XLA Modules:
  0.0 793.3 jit_solution(5334049650116615078)
XLA Ops:
  7.2 0.0 all-gather.9.cloned.1.call-start
  7.2 0.7 all-gather.9.cloned.1.call-update
  7.9 0.0 all-gather.7.cloned.1.call-start
  7.9 0.7 all-gather.7.cloned.1.call-update
  8.6 0.0 all-gather.11.cloned.1.call-start
  8.7 1.1 fusion.12
  9.8 6.2 collective-permute-start
  16.0 1.9 collective-permute-start.1
  18.0 1.6 fusion.13
  29.3 0.0 collective-permute-done
  29.3 0.0 collective-permute-done.1
  29.4 24.5 %concatenate.3 = bf16[2306,1024]{1,0:T(8,128)(2,1)} concatenate(bf16[129,1024]{1,0:T(8,128)(2,1)S(1)} %collective-permute-done, bf16[2048,1024]{1,0:T(8,128)(2,1)} %param.8, bf16[129,1024]{1,0:T(8,128)(2,1)S(1)} %collective-permute-done.1), dimensions={0} | concatenate | bytes 9445376 | tf_op jit(solution)/shard_map/concatenate | solution.py:21
  53.8 19.5 %subtract_convert_fusion = bf16[2048,1024]{1,0:T(8,128)(2,1)} fusion(bf16[2048,1024]{1,0:T(8,128)(2,1)} %param.8, bf16[2306,1024]{1,0:T(8,128)(2,1)} %concatenate.3, s32[]{:T(128)S(6)} %select_n.37, s32[]{:T(128)S(6)} %select_n.36, s32[]{:T(128)S(6)} %select_n.35, s32[]{:T(128)S(6)} %select_n.34, s32[]{:T(128)S(6)} %select_n.33, s32[]{:T(128)S(6)} %select_n.32, ...), kind=kLoop, calls=%fused_computation.9 | loop fusion | flops 39845888 | bytes 41943072 | tf_op jit(solution)/shard_map/convert_element_type | solution.py:37
  73.3 0.0 copy-start.3
  73.3 0.0 copy-start.5
  73.3 0.0 all-gather.9.cloned.1.call-done
  73.4 0.0 copy-start.2
  73.4 22.1 %all-gather.7.cloned.1.call-done = bf16[512,2048]{1,0:T(8,128)(2,1)} async-done(((bf16[64,2048]{1,0:T(8,128)(2,1)}), bf16[512,2048]{1,0:T(8,128)(2,1)}) %all-gather.7.cloned.1.call-update) | async-done | bytes 2097168 | tf_op jit(solution)/shard_map/all_gather | solution.py:56
  95.5 9.9 %convolution_bitcast_fusion = f32[512,1024]{0,1:T(8,128)} fusion(bf16[512,2048]{1,0:T(8,128)(2,1)} %all-gather.7.cloned.1.call-done, bf16[2048,1024]{1,0:T(8,128)(2,1)} %subtract_convert_fusion, bf16[512,1024]{1,0:T(8,128)(2,1)} %all-gather.9.cloned.1.call-done), kind=kOutput, calls=%fused_computation.13 | convolution fusion | flops 4303355904 | bytes 9437184 | tf_op jit(solution)/shard_map/dot_general | solution.py:66
  105.4 0.0 all-gather.11.cloned.1.call-update
  105.4 0.2 all-reduce.3.cloned.1.call-start
  105.7 0.0 copy-done.3
  105.7 0.0 copy-done.5
  105.7 0.0 copy-done.2
  105.7 0.5 copy.12
  106.3 191.8 %all-gather.11.cloned.1.call-done = f32[8192,1024]{0,1:T(8,128)} async-done(((f32[512,1024]{0,1:T(8,128)}), f32[8192,1024]{0,1:T(8,128)}) %all-gather.11.cloned.1.call-update) | async-done | bytes 33554448 | tf_op jit(solution)/shard_map/all_gather | solution.py:65
  298.1 34.9 %copy.17 = f32[128,8,16,512]{3,2,1,0:T(8,128)S(1)} copy(f32[128,8,16,512]{3,1,2,0:T(8,128)} %bitcast.41) | data formatting | bytes 67108864
  333.0 8.3 %bitcast_reduce_fusion = f32[512,1024]{0,1:T(8,128)S(1)} fusion(f32[128,8,16,512]{3,2,1,0:T(8,128)S(1)} %copy.17), kind=kLoop, calls=%fused_computation | loop fusion | flops 7864320 | bytes 35651584 | tf_op jit(solution)/shard_map/reduce_sum | solution.py:64
  341.3 0.5 subtract_convert_fusion.3
  341.8 9.8 %fusion.6 = f32[512,2048]{1,0:T(8,128)} fusion(bf16[512,1024]{0,1:T(8,128)(2,1)S(1)} %subtract_convert_fusion.3, bf16[2048,1024]{1,0:T(8,128)(2,1)} %subtract_convert_fusion, bf16[512,2048]{1,0:T(8,128)(2,1)} %all-gather.7.cloned.1.call-done), kind=kOutput, calls=%fused_computation.16 | convolution fusion | flops 4303355904 | bytes 11534336 | tf_op jit(solution)/shard_map/dot_general | solution.py:75
  351.6 0.0 copy-start.4
  351.6 0.0 copy-start.6
  351.6 0.0 all-reduce.3.cloned.1.call-update
  351.6 0.3 all-gather.13.cloned.1.call-start
  351.9 0.4 copy-done.4
  352.2 0.0 copy-done.6
  352.3 102.2 %all-reduce.3.cloned.1.call-done = f32[512,2048]{1,0:T(8,128)} async-done(((f32[512,2048]{1,0:T(8,128)}), f32[512,2048]{1,0:T(8,128)}) %all-reduce.3.cloned.1.call-update) | async-done | bytes 4194320 | tf_op jit(solution)/shard_map/psum | solution.py:78
  454.5 3.9 subtract_convert_fusion.1
  458.3 0.0 copy-start
  458.3 9.3 %fusion.5 = f32[512,1024]{1,0:T(8,128)} fusion(bf16[512,2048]{1,0:T(8,128)(2,1)S(1)} %subtract_convert_fusion.1, bf16[2048,1024]{1,0:T(8,128)(2,1)} %subtract_convert_fusion, bf16[512,1024]{0,1:T(8,128)(2,1)S(1)} %subtract_convert_fusion.3), kind=kOutput, calls=%fused_computation.15 | convolution fusion | flops 4303355904 | bytes 9437184 | tf_op jit(solution)/shard_map/dot_general | solution.py:66
  467.6 0.0 copy-done
  467.6 0.0 all-gather.13.cloned.1.call-update
  467.7 0.0 all-reduce.5.cloned.1.call-start
  467.7 186.9 %all-gather.13.cloned.1.call-done = f32[8192,1024]{1,0:T(8,128)} async-done(((f32[512,1024]{1,0:T(8,128)}), f32[8192,1024]{1,0:T(8,128)}) %all-gather.13.cloned.1.call-update) | async-done | bytes 33554448 | tf_op jit(solution)/shard_map/all_gather | solution.py:65
  654.6 12.1 %reduce_sum.19 = f32[512,1024]{1,0:T(8,128)S(1)} reduce(f32[16,512,1024]{2,1,0:T(8,128)} %bitcast.40, f32[]{:T(128)} %constant.49.clone.1), dimensions={0}, to_apply=%region_2.3 | reduce | flops 7864320 | bytes 35651588 | tf_op jit(solution)/shard_map/reduce_sum | solution.py:64
  666.7 1.8 copy.14
  668.5 0.0 copy-start.1
  668.5 3.3 subtract_convert_fusion.2
  671.8 0.0 copy-done.1
  671.8 9.9 %fusion.4 = f32[512,2048]{1,0:T(8,128)} fusion(bf16[512,1024]{0,1:T(8,128)(2,1)} %subtract_convert_fusion.2, bf16[2048,1024]{1,0:T(8,128)(2,1)} %subtract_convert_fusion, bf16[512,2048]{1,0:T(8,128)(2,1)S(1)} %copy-done.1), kind=kOutput, calls=%fused_computation.14 | convolution fusion | flops 4303355904 | bytes 11534336 | tf_op jit(solution)/shard_map/dot_general | solution.py:75
  681.6 0.0 all-reduce.5.cloned.1.call-update
  681.7 0.1 dynamic-slice
  681.8 0.1 dynamic-slice.1
  681.8 0.1 dynamic-slice.2
  681.9 1.1 constant_dynamic-slice_fusion
  683.0 0.8 copy.15
  683.7 100.8 %all-reduce.5.cloned.1.call-done = f32[512,2048]{1,0:T(8,128)} async-done(((f32[512,2048]{1,0:T(8,128)}), f32[512,2048]{1,0:T(8,128)}) %all-reduce.5.cloned.1.call-update) | async-done | bytes 4194320 | tf_op jit(solution)/shard_map/psum | solution.py:78
  784.5 1.9 subtract_convert_fusion.4
  (4 shorter events, 0.0 us)
Async XLA Ops:
  7.2 66.2 %all-gather.9.cloned.1.call-start = ((), (), s32[]{:S(2)}) async-start(), calls=%async_computation.1 | async-start | bytes 1114112 | tf_op jit(solution)/shard_map/all_gather | solution.py:57
  7.9 87.6 %all-gather.7.cloned.1.call-start = ((), (), s32[]{:S(2)}) async-start(), calls=%async_computation | async-start | bytes 2359296 | tf_op jit(solution)/shard_map/all_gather | solution.py:56
  8.6 289.4 %all-gather.11.cloned.1.call-start = ((), (), s32[]{:S(2)}) async-start(), calls=%async_computation.4 | async-start | bytes 35651584 | tf_op jit(solution)/shard_map/all_gather | solution.py:65
  9.8 19.5 %collective-permute-start = (bf16[129,1024]{1,0:T(8,128)(2,1)S(1)}, bf16[129,1024]{1,0:T(8,128)(2,1)S(1)}, u32[]{:S(2)}, u32[]{:S(2)}) collective-permute-start(bf16[129,1024]{1,0:T(8,128)(2,1)S(1)} %get-tuple-element.7), channel_id=1, source_target_pairs={{0,8},{8,16},{16,24},{24,32},{32,40},{40,48},{48,56},{56,64},{64,7... | collective-permute-start | bytes 792584 | tf_op jit(solution)/shard_map/ppermute | solution.py:19
  16.0 13.3 %collective-permute-start.1 = (bf16[129,1024]{1,0:T(8,128)(2,1)S(1)}, bf16[129,1024]{1,0:T(8,128)(2,1)S(1)}, u32[]{:S(2)}, u32[]{:S(2)}) collective-permute-start(bf16[129,1024]{1,0:T(8,128)(2,1)S(1)} %get-tuple-element.6), channel_id=1, source_target_pairs={{8,0},{16,8},{24,16},{32,24},{40,32},{48,40},{56,48},{64,56},{72,6... | collective-permute-start | bytes 792584 | tf_op jit(solution)/shard_map/ppermute | solution.py:20
  73.3 32.3 %copy-start.3 = (f32[512]{0:T(512)S(1)}, f32[512]{0:T(512)}, u32[]{:S(2)}) copy-start(f32[512]{0:T(512)} %param.15) | copy-start | bytes 6148
  73.3 32.4 %copy-start.5 = (f32[512]{0:T(512)S(1)}, f32[512]{0:T(512)}, u32[]{:S(2)}) copy-start(f32[512]{0:T(512)} %param.13) | copy-start | bytes 6148
  73.4 32.3 %copy-start.2 = (bf16[512,1024]{1,0:T(8,128)(2,1)S(1)}, bf16[512,1024]{1,0:T(8,128)(2,1)}, u32[]{:S(2)}) copy-start(bf16[512,1024]{1,0:T(8,128)(2,1)} %all-gather.9.cloned.1.call-done) | copy-start | bytes 3145732
  105.4 349.0 %all-reduce.3.cloned.1.call-start = ((), (), s32[]{:S(2)}) async-start(), calls=%async_computation.2 | async-start | bytes 8388608 | tf_op jit(solution)/shard_map/psum | solution.py:78
  351.6 0.7 copy-start.4
  351.6 0.7 copy-start.6
  351.6 303.0 %all-gather.13.cloned.1.call-start = ((), (), s32[]{:S(2)}) async-start(), calls=%async_computation.5 | async-start | bytes 35651584 | tf_op jit(solution)/shard_map/all_gather | solution.py:65
  458.3 9.3 %copy-start = (bf16[512,2048]{1,0:T(8,128)(2,1)}, bf16[512,2048]{1,0:T(8,128)(2,1)S(1)}, u32[]{:S(2)}) copy-start(bf16[512,2048]{1,0:T(8,128)(2,1)S(1)} %subtract_convert_fusion.1) | copy-start | bytes 6291460
  467.7 316.9 %all-reduce.5.cloned.1.call-start = ((), (), s32[]{:S(2)}) async-start(), calls=%async_computation.3 | async-start | bytes 8388608 | tf_op jit(solution)/shard_map/psum | solution.py:78
  668.5 3.3 copy-start.1
Sparse Core Ops, SparseCore 0:
  10.4 48.5 all-gather.8
  60.6 34.7 all-gather.6
  105.5 192.4 all-gather.10
  351.7 102.6 all-reduce.2
  467.8 186.7 all-gather.12
  681.8 102.6 all-reduce.4
